TPU v7x, 256 devices: a whole 4x4x8 slice. The times are simulated.
256 devices in a mesh: replica: 64 (over z_hi, y, x), fsdp: 4 (over z_lo, core).
Axes of the slice: x: 4, y: 4, z: 8 (z_hi: 4, z_lo: 2; z = z_hi * 2 + z_lo), core: 2. Of those that a mesh axis runs over, the one named last changes fastest.
Arguments:
- inputs: bfloat16 [32768, 2048], P(('replica', 'fsdp')), may hold values from -6 to 6
- weights: bfloat16 [131072, 4608], P('replica', 'fsdp'), may hold values from -1.155 to 1.155
- cotangent: bfloat16 [32768, 4608], P('replica', 'fsdp'), may hold values from -6 to 6
- gain: float32 [4608], P('fsdp'), may hold values from -0.5 to 1
- snapshot: bfloat16 [8192, 4608], P('replica', 'fsdp'), may hold values from -3 to 3
- global_rows: float32 [128, 4608], P(None, 'fsdp'), may hold values from -3 to 3
- momentum: float32 [128, 4608], P(None, 'fsdp'), may hold values from -3 to 3
- plan: int32 [16], replicated, may hold values from 0 to 15, as said below
- delay: int32 [1], replicated, may hold values from 1 to 15
Outputs:
- new_weights: bfloat16 [131072, 4608], P('replica', 'fsdp')
- new_global: float32 [128, 4608], P(None, 'fsdp')
- new_momentum: float32 [128, 4608], P(None, 'fsdp')
Inputs may be any that keep to these rules, and one draw needn't show every extreme that they name: `plan`: the 16 entries are distinct fragment ids.
All inputs are finite; a program needn't handle non-finite values.
Results may differ from a plain program's by a relative error of at most 0.0042.
Values may be sent and summed in bfloat16 or wider, within the bound.
A program may use at most 128 MiB of HBM per device.

v0:
```python
import jax
import jax.numpy as jnp
from jax import lax
from jax.sharding import PartitionSpec as P

norm_eps = 1e-06
inner_rate = 0.02
outer_rate = 0.7
outer_beta = 0.9
merge_weight = 0.5


def outer_part(snapshot, global_rows, momentum):
    replicas = lax.axis_size("replica")
    drift = global_rows - snapshot.astype(jnp.float32)
    summed = lax.psum(drift, "replica")
    outer_grad = summed / replicas
    new_momentum = outer_beta * momentum + outer_grad
    new_global = global_rows - outer_rate * (outer_grad + outer_beta * new_momentum)
    return (new_global, new_momentum)


def inner_part(inputs, weights, cotangent, gain):
    width = lax.axis_size("fsdp") * weights.shape[1]
    gain_factor = 1.0 + gain
    gathered = lax.all_gather(inputs, "fsdp", axis=0, tiled=True)
    proj = jnp.dot(gathered, weights, preferred_element_type=jnp.float32)
    scaled = cotangent.astype(jnp.float32) * gain_factor[None, :]
    square_sum, cross_sum = lax.psum(
        (jnp.sum(proj * proj, axis=1), jnp.sum(scaled * proj, axis=1)), "fsdp"
    )
    inverse = lax.rsqrt(square_sum / width + norm_eps)
    project_dot = cross_sum / width
    dproj = (inverse[:, None] * scaled - proj * (inverse**3 * project_dot)[:, None]).astype(
        jnp.bfloat16
    )
    contract = (((0,), (0,)), ((), ()))
    grad = lax.dot_general(gathered, dproj, contract, preferred_element_type=jnp.float32)
    return weights.astype(jnp.float32) - inner_rate * grad


def local(inputs, weights, cotangent, gain, snapshot, global_rows, momentum, plan, delay):
    stepped = inner_part(inputs, weights, cotangent, gain)
    new_global, new_momentum = outer_part(snapshot, global_rows, momentum)
    frag_height = global_rows.shape[0]
    position = plan.shape[0] - 1 - delay[0]
    fragment = lax.dynamic_index_in_dim(plan, position, 0, keepdims=False)
    first_row = fragment * frag_height
    chosen = lax.dynamic_slice_in_dim(stepped, first_row, frag_height, 0)
    mixed = (1.0 - merge_weight) * chosen + merge_weight * new_global
    merged = lax.dynamic_update_slice_in_dim(stepped, mixed, first_row, 0)
    return (merged.astype(jnp.bfloat16), new_global, new_momentum)


def solution(mesh):
    in_specs = (
        P(("replica", "fsdp"), None),
        P("replica", "fsdp"),
        P("replica", "fsdp"),
        P("fsdp"),
        P("replica", "fsdp"),
        P(None, "fsdp"),
        P(None, "fsdp"),
        P(),
        P(),
    )
    out_specs = (P("replica", "fsdp"), P(None, "fsdp"), P(None, "fsdp"))
    return jax.shard_map(local, mesh=mesh, in_specs=in_specs, out_specs=out_specs, check_vma=False)
```

profile of v0, /device:TPU:2, one launch (start us, length us, event | category | flops | bytes accessed | tf_op | source)
XLA Modules:
  0.0 729.5 jit_solution(7022525957317789440)
XLA Ops:
  8.0 0.0 copy-start.2
  8.0 0.0 copy-start.1
  8.0 0.0 copy-start
  8.0 0.0 all-gather.2.cloned.1.call-start
  8.1 0.7 all-gather.2.cloned.1.call-update
  8.8 0.0 all-reduce.3.cloned.1.call-start
  8.8 1.2 copy.13
  10.0 1.3 copy.16
  11.3 0.9 convert_subtract_fusion
  12.2 0.0 all-reduce.3.cloned.1.call-update
  12.8 0.0 copy-done.2
  12.8 0.6 dynamic_slice.7
  14.1 0.0 copy-done.1
  14.1 0.0 copy-done
  14.1 0.2 copy.15
  14.3 6.6 copy.12
  21.0 24.2 %all-gather.2.cloned.1.call-done = bf16[512,2048]{1,0:T(8,128)(2,1)} async-done(((bf16[128,2048]{1,0:T(8,128)(2,1)}), bf16[512,2048]{1,0:T(8,128)(2,1)}) %all-gather.2.cloned.1.call-update) | async-done | bytes 2097168 | tf_op jit(solution)/shard_map/all_gather | solution.py:26
  45.2 6.4 multiply_reduce_fusion.1
  51.6 6.8 all-reduce
  58.3 0.7 add_rsqrt_fusion
  59.0 9.8 %bitcast_subtract_fusion = f32[2048,1152]{0,1:T(8,128)} fusion(bf16[2048,1152]{0,1:T(8,128)(2,1)} %copy.12, bf16[512,2048]{1,0:T(8,128)(2,1)} %all-gather.2.cloned.1.call-done, f32[512,1152]{1,0:T(8,128)S(1)} %get-tuple-element.15, bf16[512,1152]{1,0:T(8,128)(2,1)} %param.11, f32[512]{0:T(512)S(1)} %get-tuple-element.14, f32[1152]{0:T(1024)S(1)} %broadcast_add_fusion, ...), kind=kOutput, calls=%fused_computation.1 | convolution fusion | flops 2426535936 | bytes 19800576 | tf_op jit(solution)/shard_map/dot_general | solution.py:38
  68.9 635.6 %all-reduce.3.cloned.1.call-done = f32[128,1152]{0,1:T(8,128)} async-done(((f32[128,1152]{0,1:T(8,128)}), f32[128,1152]{0,1:T(8,128)}) %all-reduce.3.cloned.1.call-update) | async-done | bytes 589840 | tf_op jit(solution)/shard_map/psum | solution.py:16
  704.4 2.3 multiply_dynamic-update-slice_fusion
  706.7 6.7 convert_element_type.19
  713.4 6.6 copy.17
  720.0 1.0 copy.18
  721.1 1.0 copy.19
  (1 shorter events, 0.0 us)
Async XLA Ops:
  8.0 4.8 copy-start.2
  8.0 6.1 copy-start.1
  8.0 6.1 copy-start
  8.0 37.2 %all-gather.2.cloned.1.call-start = ((), (), s32[]{:S(2)}) async-start(), calls=%async_computation | async-start | bytes 2621440 | tf_op jit(solution)/shard_map/all_gather | solution.py:26
  8.8 695.6 %all-reduce.3.cloned.1.call-start = ((), (), s32[]{:S(2)}) async-start(), calls=%async_computation.1 | async-start | bytes 1179648 | tf_op jit(solution)/shard_map/psum | solution.py:16
Sparse Core Ops, SparseCore 0:
  10.7 34.4 all-gather.1
Sparse Core Ops, SparseCore 1:
  12.4 691.9 all-reduce.2
where the time goes:
time: 730 us
  waiting for transfers between devices  661 us (91%)
  local copies, waits for them, and re-layouts  18.6 us (3%)
  between operations  16.8 us (2%)
  matrix products  16.2 us (2%)
  other arithmetic  10.6 us (1%)
    psum x1, waiting for transfers between devices, outer_part(): summed = lax.psum(drift, 'replica')  636 us
    all_gather x1, waiting for transfers between devices, inner_part(): gathered = lax.all_gather(inputs, 'fsdp', axis=0, tiled=True)  24.2 us
    unnamed x13, local copies, waits for them, and re-layouts  18 us
  transfers between devices with their start and end apart: 2, of which 2 were waited for; matrix products, arithmetic and copies ran while one was open for 4% of the time, Pallas kernels for 0%

commit v1 on v0

v1 whole, which is shorter than its diff:
```python
import functools

import jax
import jax.numpy as jnp
from jax import lax
from jax.experimental import pallas as pl
from jax.experimental.pallas import tpu as pltpu
from jax.sharding import PartitionSpec as P

norm_eps = 1e-06
inner_rate = 0.02
outer_rate = 0.7
outer_beta = 0.9
merge_weight = 0.5

GRID = (4, 4, 4)
CHUNKS = 4

f32 = jnp.float32
bf16 = jnp.bfloat16


def split_columns(width):
    first = (width // 128 + 1) // 2 * 128
    return ((0, first), (first, width))


def exchange_kernel(
    x_hbm, w_hbm, cot_hbm, gain_ref, snap_hbm, global_hbm, momentum_hbm,
    w_ref, xt_ref, dproj_ref, new_global_ref, new_momentum_ref,
    xbuf, cot, proj, message, sums, total, old_global, old_momentum,
    snap_a, snap_b, part_a, part_b, have_a, have_b, plane_a, plane_b,
    local_sem, sib_send, sib_recv, far_send, far_recv, fwd_send, fwd_recv,
    sum_send, sum_recv, outer_send, outer_recv,
):
    nz, ny, nx = GRID
    replicas = nz * ny * nx
    r = lax.axis_index("replica")
    f = lax.axis_index("fsdp")
    x = lax.rem(r, nx)
    y = lax.rem(lax.div(r, nx), ny)
    z = lax.div(r, nx * ny)
    core = lax.rem(f, 2)
    sibling = f + 1 - 2 * core
    far = lax.rem(f + 2, 4)
    far_sibling = 3 - f
    _, chunks, step, _ = xbuf.shape
    rows = 4 * step
    width = w_ref.shape[1]
    model = 4 * width

    def x_peer(d):
        return {"replica": r - x + lax.rem(x + d, nx)}

    def y_peer(d):
        return {"replica": r + nx * (lax.rem(y + d, ny) - y)}

    def z_peer(d):
        return {"replica": r + nx * ny * (lax.rem(z + d, nz) - z)}

    def fsdp_peer(which):
        return {"fsdp": which}

    sent = []

    def remote(src, dst, send, recv, where):
        copy = pltpu.make_async_remote_copy(
            src_ref=src, dst_ref=dst, send_sem=send, recv_sem=recv,
            device_id=where, device_id_type=pl.DeviceIdType.MESH,
        )
        sent.append(copy)
        return copy

    cut_a, cut_b = split_columns(width)
    halves = (
        (cut_a, (x, nx, x_peer), (y, ny, y_peer), snap_a, part_a, have_a, plane_a),
        (cut_b, (y, ny, y_peer), (x, nx, x_peer), snap_b, part_b, have_b, plane_b),
    )
    height = total.shape[0]

    mine = [
        pltpu.make_async_copy(x_hbm, xbuf.at[f], local_sem.at[0]),
        pltpu.make_async_copy(w_hbm, w_ref, local_sem.at[1]),
        pltpu.make_async_copy(cot_hbm, cot, local_sem.at[2]),
        pltpu.make_async_copy(global_hbm, old_global, local_sem.at[3]),
        pltpu.make_async_copy(momentum_hbm, old_momentum, local_sem.at[4]),
    ]
    own_snap = []
    for h, ((lo, hi), (i, n, _), _, snaps, _, _, _) in enumerate(halves):
        block = height // n
        own_snap.append(
            pltpu.make_async_copy(
                snap_hbm.at[pl.ds(i * block, block), pl.ds(lo, hi - lo)],
                snaps.at[n - 1],
                local_sem.at[5 + h],
            )
        )

    barrier = pltpu.get_barrier_semaphore()
    partners = [fsdp_peer(sibling), fsdp_peer(far), fsdp_peer(far_sibling)]
    partners += [x_peer(d) for d in range(1, nx)]
    partners += [y_peer(d) for d in range(1, ny)]
    partners += [z_peer(d) for d in range(1, nz)]
    for where in partners:
        pl.semaphore_signal(barrier, inc=1, device_id=where, device_id_type=pl.DeviceIdType.MESH)
    for copy in mine + own_snap:
        copy.start()
    pl.semaphore_wait(barrier, len(partners))

    far_copy, sib_copy, fwd_copy = [], [], []
    for c in range(chunks):
        far_copy.append(
            remote(x_hbm.at[c], xbuf.at[f, c], far_send.at[c], far_recv.at[c], fsdp_peer(far))
        )
        sib_copy.append(
            remote(x_hbm.at[c], xbuf.at[f, c], sib_send.at[c], sib_recv.at[c], fsdp_peer(sibling))
        )
        far_copy[c].start()
        sib_copy[c].start()

    def scatter_first(h):
        (lo, hi), (i, n, peer), _, snaps, _, _, _ = halves[h]
        block = height // n
        copies = []
        for d in range(1, n):
            there = lax.rem(i + d, n)
            copies.append(
                remote(
                    snap_hbm.at[pl.ds(there * block, block), pl.ds(lo, hi - lo)],
                    snaps.at[d - 1],
                    outer_send.at[0, h, d - 1], outer_recv.at[0, h, d - 1], peer(d),
                )
            )
        for copy in copies:
            copy.start()
        return copies

    def scatter_second(h, before):
        _, (_, n, _), (j, m, peer), snaps, part, have, _ = halves[h]
        for copy in before:
            copy.wait_recv()
        own_snap[h].wait()
        amount = snaps[0].astype(f32)
        for k in range(1, n):
            amount += snaps[k].astype(f32)
        part[...] = amount
        size = part.shape[0] // m
        copies = []
        for d in range(1, m):
            there = lax.rem(j + d, m)
            copies.append(
                remote(
                    part.at[pl.ds(there * size, size)], have.at[d - 1],
                    outer_send.at[1, h, d - 1], outer_recv.at[1, h, d - 1], peer(d),
                )
            )
        for copy in copies:
            copy.start()
        return copies

    def across_planes(h, before):
        _, _, (j, m, _), _, part, have, plane = halves[h]
        for copy in before:
            copy.wait_recv()
        size = part.shape[0] // m
        amount = part[pl.ds(pl.multiple_of(j * size, size), size), :]
        for k in range(m - 1):
            amount += have[k]
        plane[z] = amount
        copies = []
        for d in range(1, nz):
            copies.append(
                remote(
                    plane.at[z], plane.at[z],
                    outer_send.at[2, h, d - 1], outer_recv.at[2, h, d - 1], z_peer(d),
                )
            )
        for copy in copies:
            copy.start()
        return copies

    def gather_second(h, before):
        (lo, hi), (i, n, _), (j, m, peer), _, _, _, plane = halves[h]
        for copy in before:
            copy.wait_recv()
        amount = plane[0]
        for k in range(1, nz):
            amount += plane[k]
        size = height // (n * m)
        here = pl.ds(pl.multiple_of((i * m + j) * size, size), size)
        total[here, lo:hi] = amount
        copies = []
        for d in range(1, m):
            place = total.at[here, pl.ds(lo, hi - lo)]
            copies.append(
                remote(place, place, outer_send.at[3, h, d - 1], outer_recv.at[3, h, d - 1], peer(d))
            )
        for copy in copies:
            copy.start()
        return copies

    def gather_first(h, before):
        (lo, hi), (i, n, peer), _, _, _, _, _ = halves[h]
        for copy in before:
            copy.wait_recv()
        block = height // n
        copies = []
        for d in range(1, n):
            place = total.at[pl.ds(i * block, block), pl.ds(lo, hi - lo)]
            copies.append(
                remote(place, place, outer_send.at[4, h, d - 1], outer_recv.at[4, h, d - 1], peer(d))
            )
        for copy in copies:
            copy.start()
        return copies

    stages = (scatter_second, across_planes, gather_second, gather_first)
    outer = [scatter_first(h) for h in range(2)]
    gain_factor = 1.0 + gain_ref[...]

    def scaled_of(c):
        return cot[:, c].reshape(rows, width).astype(f32) * gain_factor

    def lanes(value):
        amount = value[:, :128]
        for k in range(128, width, 128):
            amount += value[:, k : k + 128]
        return jnp.sum(amount.T, axis=0, keepdims=True)

    def project(c):
        tokens = xbuf[:, c].reshape(rows, xbuf.shape[3])
        value = jnp.dot(tokens, w_ref[...], preferred_element_type=f32)
        proj[c] = value
        message[c, 0:1, :] = lanes(value * value)
        message[c, 1:2, :] = lanes(scaled_of(c) * value)
        copies = []
        for d, where in enumerate((sibling, far, far_sibling)):
            copies.append(
                remote(
                    message.at[c], sums.at[c, d],
                    sum_send.at[c, d], sum_recv.at[c, d], fsdp_peer(where),
                )
            )
        for copy in copies:
            copy.start()
        xt_ref[:, c * rows : (c + 1) * rows] = tokens.T
        return copies

    def column(value):
        return jnp.broadcast_to(value, (128, rows)).T

    def finish(c, before):
        for copy in before:
            copy.wait_recv()
        both = message[c] + sums[c, 0] + sums[c, 1] + sums[c, 2]
        inverse = lax.rsqrt(both[0:1] / model + norm_eps)
        factor = inverse * inverse * inverse * (both[1:2] / model)
        inverse, factor = column(inverse), column(factor)
        scaled = scaled_of(c)
        for k in range(0, width, 128):
            value = inverse * scaled[:, k : k + 128] - proj[c, :, k : k + 128] * factor
            dproj_ref[c * rows : (c + 1) * rows, k : k + 128] = value.astype(bf16)

    message[...] = jnp.zeros_like(message)
    pending = None
    for c in range(chunks):
        far_copy[c].wait_recv()
        fwd_copy.append(
            remote(
                xbuf.at[far, c], xbuf.at[far, c], fwd_send.at[c], fwd_recv.at[c], fsdp_peer(sibling)
            )
        )
        fwd_copy[c].start()
        outer = [stages[c](h, outer[h]) for h in range(2)]
        if c == 0:
            for copy in mine[:3]:
                copy.wait()
        sib_copy[c].wait_recv()
        fwd_copy[c].wait_recv()
        now = project(c)
        if pending is not None:
            finish(c - 1, pending)
        pending = now
    finish(chunks - 1, pending)
    for h in range(2):
        for copy in outer[h]:
            copy.wait_recv()
    for copy in mine[3:]:
        copy.wait()
    outer_grad = old_global[...] - total[...] / replicas
    new_momentum = outer_beta * old_momentum[...] + outer_grad
    new_momentum_ref[...] = new_momentum
    new_global_ref[...] = old_global[...] - outer_rate * (outer_grad + outer_beta * new_momentum)
    for copy in sent:
        copy.wait_send()


def update_kernel(
    plan_ref, delay_ref, w_ref, xt_ref, dproj_ref, new_global_ref, new_momentum_ref,
    out_hbm, global_hbm, momentum_hbm, tile, tile_sem, outer_sem,
):
    slots, step, _ = tile.shape
    height = new_global_ref.shape[0]
    steps = w_ref.shape[0] // step
    fragment = plan_ref[plan_ref.shape[0] - 1 - delay_ref[0]]
    outer = [
        pltpu.make_async_copy(new_global_ref, global_hbm, outer_sem.at[0]),
        pltpu.make_async_copy(new_momentum_ref, momentum_hbm, outer_sem.at[1]),
    ]
    for copy in outer:
        copy.start()
    copies = []
    for i in range(steps):
        slot = i % slots
        if i >= slots:
            copies[i - slots].wait()
        here = slice(i * step, (i + 1) * step)
        grad = jnp.dot(xt_ref[here], dproj_ref[...], preferred_element_type=f32)
        stepped = w_ref[here].astype(f32) - inner_rate * grad
        tile[slot] = stepped.astype(bf16)
        for k in range(step // height):

            @pl.when(fragment == i * (step // height) + k)
            def _():
                part = slice(k * height, (k + 1) * height)
                chosen = stepped[part]
                mixed = (1.0 - merge_weight) * chosen + merge_weight * new_global_ref[...]
                tile[slot, part] = mixed.astype(bf16)

        copies.append(
            pltpu.make_async_copy(tile.at[slot], out_hbm.at[pl.ds(i * step, step)], tile_sem.at[slot])
        )
        copies[i].start()
    for copy in copies[max(steps - slots, 0) :] + outer:
        copy.wait()


def local(inputs, weights, cotangent, gain, snapshot, global_rows, momentum, plan, delay):
    tokens, features = inputs.shape
    width = weights.shape[1]
    height = snapshot.shape[0]
    chunks = CHUNKS
    step = tokens // chunks
    nz, ny, nx = GRID
    cut_a, cut_b = split_columns(width)
    wide_a, wide_b = cut_a[1] - cut_a[0], cut_b[1] - cut_b[0]
    size = height // (nx * ny)
    most = max(nx, ny, nz)
    hbm = pl.BlockSpec(memory_space=pltpu.HBM)
    vmem = pl.BlockSpec(memory_space=pltpu.VMEM)
    smem = pl.BlockSpec(memory_space=pltpu.SMEM)
    dma = pltpu.SemaphoreType.DMA
    kept = pl.pallas_call(
        exchange_kernel,
        name="exchange",
        out_shape=(
            pltpu.VMEM((features, width), bf16),
            pltpu.VMEM((features, 4 * tokens), bf16),
            pltpu.VMEM((4 * tokens, width), bf16),
            pltpu.VMEM((height, width), f32),
            pltpu.VMEM((height, width), f32),
        ),
        in_specs=[hbm, hbm, hbm, vmem, hbm, hbm, hbm],
        out_specs=(vmem,) * 5,
        scratch_shapes=[
            pltpu.VMEM((4, chunks, step, features), bf16),
            pltpu.VMEM((4, chunks, step, width), bf16),
            pltpu.VMEM((chunks, 4 * step, width), f32),
            pltpu.VMEM((chunks, 8, 4 * step), f32),
            pltpu.VMEM((chunks, 3, 8, 4 * step), f32),
            pltpu.VMEM((height, width), f32),
            pltpu.VMEM((height, width), f32),
            pltpu.VMEM((height, width), f32),
            pltpu.VMEM((nx, height // nx, wide_a), bf16),
            pltpu.VMEM((ny, height // ny, wide_b), bf16),
            pltpu.VMEM((height // nx, wide_a), f32),
            pltpu.VMEM((height // ny, wide_b), f32),
            pltpu.VMEM((ny - 1, size, wide_a), f32),
            pltpu.VMEM((nx - 1, size, wide_b), f32),
            pltpu.VMEM((nz, size, wide_a), f32),
            pltpu.VMEM((nz, size, wide_b), f32),
            dma((7,)),
            dma((chunks,)),
            dma((chunks,)),
            dma((chunks,)),
            dma((chunks,)),
            dma((chunks,)),
            dma((chunks,)),
            dma((chunks, 3)),
            dma((chunks, 3)),
            dma((5, 2, most - 1)),
            dma((5, 2, most - 1)),
        ],
        compiler_params=pltpu.CompilerParams(
            collective_id=0, has_side_effects=True, vmem_limit_bytes=32 * 2**20
        ),
    )(
        inputs.reshape(chunks, step, features),
        weights,
        cotangent.reshape(4, chunks, step, width),
        gain.reshape(1, width),
        snapshot,
        global_rows,
        momentum,
    )
    kept = [pltpu.with_memory_space_constraint(value, pltpu.VMEM) for value in kept]
    block = 256 if features % 256 == 0 else 128
    return pl.pallas_call(
        update_kernel,
        name="update",
        out_shape=(
            jax.ShapeDtypeStruct((features, width), bf16),
            jax.ShapeDtypeStruct((height, width), f32),
            jax.ShapeDtypeStruct((height, width), f32),
        ),
        in_specs=[smem, smem] + [vmem] * 5,
        out_specs=(hbm,) * 3,
        scratch_shapes=[
            pltpu.VMEM((4, block, width), bf16),
            dma((4,)),
            dma((2,)),
        ],
        compiler_params=pltpu.CompilerParams(vmem_limit_bytes=24 * 2**20),
    )(plan, delay, *kept)


def solution(mesh):
    in_specs = (
        P(("replica", "fsdp"), None),
        P("replica", "fsdp"),
        P("replica", "fsdp"),
        P("fsdp"),
        P("replica", "fsdp"),
        P(None, "fsdp"),
        P(None, "fsdp"),
        P(),
        P(),
    )
    out_specs = (P("replica", "fsdp"), P(None, "fsdp"), P(None, "fsdp"))
    return jax.shard_map(local, mesh=mesh, in_specs=in_specs, out_specs=out_specs, check_vma=False)
```

time: 730 us -> 51.9 us (0.07)
  the two profiles are of different devices: /device:TPU:2 before, /device:TPU:1 now
where the time goes in v1:
time: 51.9 us; the launch traced here: 51.5 us
  Pallas kernels  41.7 us (80%)
  local copies, waits for them, and re-layouts  8.44 us (16%)
  between operations  1.32 us (3%)
    pallas_call x1, Pallas kernels, local(): pl.pallas_call(exchange_kernel, name='exchange', out_shape=(pltpu.VMEM((f...  36.1 us
    unnamed x14, local copies, waits for them, and re-layouts  7.74 us
    pallas_call x1, Pallas kernels, local(): pl.pallas_call(update_kernel, name='update', out_shape=(jax.ShapeDtypeStr...  5.65 us

profile of v1, /device:TPU:1, one launch (start us, length us, event | category | flops | bytes accessed | tf_op | source)
XLA Modules:
  0.0 51.5 jit_solution(3492260913819720616)
XLA Ops:
  0.6 0.0 copy-start.6
  1.3 0.7 %reshape.17.gain_ref = f32[1,1152]{1,0:T(1,128)S(1)} reshape(f32[1152]{0:T(1024)} %param.12) | data formatting | bytes 9216 | tf_op jit(solution)/shard_map/reshape | solution.py:401
  2.0 0.0 copy-start
  2.0 2.3 %copy-done = bf16[2048,1152]{1,0:T(8,128)(2,1)S(1)} copy-done((bf16[2048,1152]{1,0:T(8,128)(2,1)S(1)}, bf16[2048,1152]{1,0:T(8,128)(2,1)}, u32[]{:S(2)}) %copy-start) | copy-done | bytes 4718616
  4.3 0.0 copy-start.1
  4.3 1.3 %copy-done.1 = bf16[512,1152]{1,0:T(8,128)(2,1)S(1)} copy-done((bf16[512,1152]{1,0:T(8,128)(2,1)S(1)}, bf16[512,1152]{1,0:T(8,128)(2,1)}, u32[]{:S(2)}) %copy-start.1) | copy-done | bytes 1179672
  5.6 0.0 copy-start.2
  5.6 1.1 %copy-done.2 = f32[128,1152]{1,0:T(8,128)S(1)} copy-done((f32[128,1152]{1,0:T(8,128)S(1)}, f32[128,1152]{1,0:T(8,128)}, u32[]{:S(2)}) %copy-start.2) | copy-done | bytes 589848
  6.7 0.0 copy-start.3
  6.7 1.1 %copy-done.3 = f32[128,1152]{1,0:T(8,128)S(1)} copy-done((f32[128,1152]{1,0:T(8,128)S(1)}, f32[128,1152]{1,0:T(8,128)}, u32[]{:S(2)}) %copy-start.3) | copy-done | bytes 589848
  7.7 0.0 copy-start.4
  7.7 1.0 %copy-done.4 = bf16[128,2048]{1,0:T(8,128)(2,1)S(1)} copy-done((bf16[128,2048]{1,0:T(8,128)(2,1)S(1)}, bf16[128,2048]{1,0:T(8,128)(2,1)}, u32[]{:S(2)}) %copy-start.4) | copy-done | bytes 524312
  8.8 0.0 copy-start.5
  8.8 1.0 %copy-done.5 = bf16[128,1152]{1,0:T(8,128)(2,1)S(1)} copy-done((bf16[128,1152]{1,0:T(8,128)(2,1)S(1)}, bf16[128,1152]{1,0:T(8,128)(2,1)}, u32[]{:S(2)}) %copy-start.5) | copy-done | bytes 294936
  9.7 36.1 %exchange.1 = (bf16[2048,1152]{1,0:T(8,128)(2,1)S(1)}, bf16[2048,512]{1,0:T(8,128)(2,1)S(1)}, bf16[512,1152]{1,0:T(8,128)(2,1)S(1)}, f32[128,1152]{1,0:T(8,128)S(1)}, f32[128,1152]{1,0:T(8,128)S(1)}) custom-call(bf16[4,32,2048]{2,1,0:T(8,128)(2,1)S(1)} %bitcast.3, bf16[2048,1152]{1,0:T(8,128)(2,1)S(1)} %copy-done, bf16[4,4,32,1152]{3,2,1,0:T(8,128)(2,1)S(1)} %bitcast.2, ...), custom_call_target="tpu_custom_call" | custom-call | tf_op jit(solution)/shard_map/exchange/pallas_call | solution.py:353
  45.8 0.0 copy-done.6
  45.8 5.7 %update.1 = (bf16[2048,1152]{1,0:T(8,128)(2,1)}, f32[128,1152]{1,0:T(8,128)}, f32[128,1152]{1,0:T(8,128)}) custom-call(s32[16]{0:T(128)S(1)} %copy-done.6, s32[1]{0:T(128)S(6)} %copy.12.delay_ref, bf16[2048,1152]{1,0:T(8,128)(2,1)S(1)} %get-tuple-element.8.w_ref, bf16[2048,512]{1,0:T(8,128)(2,1)S(1)} %get-tuple-element.9.xt_ref, ...), custom_call_target="tpu_custom_call" | custom-call | tf_op jit(solution)/shard_map/update/pallas_call | solution.py:408
Async XLA Ops:
  0.6 45.2 %copy-start.6 = (s32[16]{0:T(128)S(1)}, s32[16]{0:T(128)}, u32[]{:S(2)}) copy-start(s32[16]{0:T(128)} %plan_ref.1) | copy-start | bytes 196
  2.0 2.3 %copy-start = (bf16[2048,1152]{1,0:T(8,128)(2,1)S(1)}, bf16[2048,1152]{1,0:T(8,128)(2,1)}, u32[]{:S(2)}) copy-start(bf16[2048,1152]{1,0:T(8,128)(2,1)} %w_hbm.1) | copy-start | bytes 14155780
  4.3 1.3 %copy-start.1 = (bf16[512,1152]{1,0:T(8,128)(2,1)S(1)}, bf16[512,1152]{1,0:T(8,128)(2,1)}, u32[]{:S(2)}) copy-start(bf16[512,1152]{1,0:T(8,128)(2,1)} %param.11) | copy-start | bytes 3538948
  5.6 1.1 %copy-start.2 = (f32[128,1152]{1,0:T(8,128)S(1)}, f32[128,1152]{1,0:T(8,128)}, u32[]{:S(2)}) copy-start(f32[128,1152]{1,0:T(8,128)} %global_hbm.1) | copy-start | bytes 1769476
  6.7 1.1 %copy-start.3 = (f32[128,1152]{1,0:T(8,128)S(1)}, f32[128,1152]{1,0:T(8,128)}, u32[]{:S(2)}) copy-start(f32[128,1152]{1,0:T(8,128)} %momentum_hbm.1) | copy-start | bytes 1769476
  7.7 1.0 %copy-start.4 = (bf16[128,2048]{1,0:T(8,128)(2,1)S(1)}, bf16[128,2048]{1,0:T(8,128)(2,1)}, u32[]{:S(2)}) copy-start(bf16[128,2048]{1,0:T(8,128)(2,1)} %param.9) | copy-start | bytes 1572868
  8.8 1.0 %copy-start.5 = (bf16[128,1152]{1,0:T(8,128)(2,1)S(1)}, bf16[128,1152]{1,0:T(8,128)(2,1)}, u32[]{:S(2)}) copy-start(bf16[128,1152]{1,0:T(8,128)(2,1)} %snap_hbm.1) | copy-start | bytes 884740

commit v2 on v0

v2 whole, which is shorter than its diff:
```python
import functools

import jax
import jax.numpy as jnp
from jax import lax
from jax.experimental import pallas as pl
from jax.experimental.pallas import tpu as pltpu
from jax.sharding import PartitionSpec as P

norm_eps = 1e-06
inner_rate = 0.02
outer_rate = 0.7
outer_beta = 0.9
merge_weight = 0.5

GRID = (4, 4, 4)
CHUNKS = 4
AHEAD = 2

f32 = jnp.float32
bf16 = jnp.bfloat16


def split_columns(width):
    first = (width // 128 + 1) // 2 * 128
    return ((0, first), (first, width))


def exchange_kernel(
    x_hbm, w_hbm, cot_hbm, gain_hbm, snap_hbm, global_hbm, momentum_hbm,
    x_ref, w_ref, dproj, stepped_ref, total, old_global, old_momentum,
    cot, gain, proj, grad, message, sums,
    snaps, plane,
    local_sem, sib_send, sib_recv, far_send, far_recv, fwd_send, fwd_recv,
    sum_send, sum_recv, scatter_send, scatter_recv, plane_send, plane_recv,
    axis_send, axis_recv, gather_send, gather_recv,
):
    nz, ny, nx = GRID
    r = lax.axis_index("replica")
    f = lax.axis_index("fsdp")
    x = lax.rem(r, nx)
    y = lax.rem(lax.div(r, nx), ny)
    z = lax.div(r, nx * ny)
    place = lax.rem(r, nx * ny)
    core = lax.rem(f, 2)
    sibling = f + 1 - 2 * core
    far = lax.rem(f + 2, 4)
    far_sibling = 3 - f
    _, chunks, step, features = x_ref.shape
    rows = 4 * step
    width = w_ref.shape[1]
    model = 4 * width
    height = total.shape[0]
    size = height // (nx * ny)
    columns = split_columns(width)

    def x_peer(d):
        return {"replica": r - x + lax.rem(x + d, nx)}

    def y_peer(d):
        return {"replica": r + nx * (lax.rem(y + d, ny) - y)}

    def plane_peer(d):
        return {"replica": r - place + lax.rem(place + d, nx * ny)}

    def z_peer(d):
        return {"replica": r + nx * ny * (lax.rem(z + d, nz) - z)}

    def fsdp_peer(which):
        return {"fsdp": which}

    sent = []

    def send(src, dst, send_sem, recv_sem, where):
        copy = pltpu.make_async_remote_copy(
            src_ref=src, dst_ref=dst, send_sem=send_sem, recv_sem=recv_sem,
            device_id=where, device_id_type=pl.DeviceIdType.MESH,
        )
        copy.start()
        sent.append(copy)
        return copy

    barrier = pltpu.get_barrier_semaphore()
    partners = [fsdp_peer(sibling), fsdp_peer(far), fsdp_peer(far_sibling)]
    partners += [plane_peer(d) for d in range(1, nx * ny)]
    partners += [z_peer(d) for d in range(1, nz)]
    for where in partners:
        pl.semaphore_signal(barrier, inc=1, device_id=where, device_id_type=pl.DeviceIdType.MESH)

    mine = []
    for which, (src, dst) in enumerate((
        (w_hbm, w_ref), (x_hbm, x_ref.at[f]), (cot_hbm, cot), (gain_hbm, gain),
        (global_hbm, old_global), (momentum_hbm, old_momentum),
    )):
        mine.append(pltpu.make_async_copy(src, dst, local_sem.at[which]))
    mine.append(pltpu.make_async_copy(snap_hbm.at[place], snaps.at[0], local_sem.at[len(mine)]))
    mine[0].start()
    pl.semaphore_wait(barrier, len(partners))

    def scatter():
        return [
            send(
                snap_hbm.at[lax.rem(place + d, nx * ny)], snaps.at[d],
                scatter_send.at[d - 1], scatter_recv.at[d - 1], plane_peer(d),
            )
            for d in range(1, nx * ny)
        ]

    def across_planes(before):
        mine[-1].wait()
        for copy in before:
            copy.wait_recv()
        amount = snaps[0].astype(f32)
        for k in range(1, nx * ny):
            amount += snaps[k].astype(f32)
        plane[z] = amount
        return [
            send(plane.at[z], plane.at[z], plane_send.at[d - 1], plane_recv.at[d - 1], z_peer(d))
            for d in range(1, nz)
        ]

    def piece(k):
        return total.at[pl.ds(pl.multiple_of(k * size, size), size)]

    axes = ((nx, x_peer), (ny, y_peer))

    def gather_axes(before):
        for copy in before:
            copy.wait_recv()
        amount = plane[0]
        for k in range(1, nz):
            amount += plane[k]
        here = piece(place)
        here[...] = amount
        return [
            [
                send(here, here, axis_send.at[a, d - 1], axis_recv.at[a, d - 1], peer(d))
                for d in range(1, n)
            ]
            for a, (n, peer) in enumerate(axes)
        ]

    def gather_rest(before):
        arriving = []
        most = max(nx, ny)
        for d in sorted(range(1, most), key=lambda d: min(d, most - d)):
            for a, (n, _) in enumerate(axes):
                if d >= n:
                    continue
                before[a][d - 1].wait_recv()
                from_x = place - x + lax.rem(x + nx - d, nx)
                from_y = place + nx * (lax.rem(y + ny - d, ny) - y)
                lo, hi = columns[1 - a]
                part = piece((from_x, from_y)[a]).at[:, pl.ds(lo, hi - lo)]
                m, peer = axes[1 - a]
                for e in range(1, m):
                    arriving.append(
                        send(
                            part, part,
                            gather_send.at[a, d - 1, e - 1], gather_recv.at[a, d - 1, e - 1], peer(e),
                        )
                    )
        return arriving

    def scaled_of(c):
        return cot[:, c].reshape(rows, width).astype(f32) * (1.0 + gain[...].reshape(1, width))

    def lanes(value):
        amount = value[:, :128]
        for k in range(128, width, 128):
            amount += value[:, k : k + 128]
        return jnp.sum(amount.T, axis=0, keepdims=True)

    def project(c):
        tokens = x_ref[:, c].reshape(rows, features)
        value = jnp.dot(tokens, w_ref[...], preferred_element_type=f32)
        proj[c] = value
        message[c, 0:1, :] = lanes(value * value)
        message[c, 1:2, :] = lanes(scaled_of(c) * value)
        return [
            send(
                message.at[c], sums.at[c, d], sum_send.at[c, d], sum_recv.at[c, d], fsdp_peer(where)
            )
            for d, where in enumerate((sibling, far, far_sibling))
        ]

    def column(value):
        return jnp.broadcast_to(value, (128, rows)).T

    def finish(c, before):
        for copy in before:
            copy.wait_recv()
        both = message[c] + sums[c, 0] + sums[c, 1] + sums[c, 2]
        inverse = lax.rsqrt(both[0:1] / model + norm_eps)
        factor = inverse * inverse * inverse * (both[1:2] / model)
        inverse, factor = column(inverse), column(factor)
        scaled = scaled_of(c)
        for k in range(0, width, 128):
            value = inverse * scaled[:, k : k + 128] - proj[c, :, k : k + 128] * factor
            dproj[:, c, :, k : k + 128] = value.astype(bf16).reshape(4, step, 128)

    def gradient(first, last, final):
        count = last - first
        right = dproj[:, first:last].reshape(count * rows, width)
        tile = min(256, features)
        for k in range(0, features, tile):
            left = x_ref[:, first:last, :, k : k + tile].reshape(count * rows, tile)
            value = lax.dot_general(
                left, right, (((0,), (0,)), ((), ())), preferred_element_type=f32
            )
            if final:
                value = w_ref[k : k + tile].astype(f32) - inner_rate * (grad[k : k + tile] + value)
                stepped_ref[k : k + tile] = value.astype(bf16)
            else:
                grad[k : k + tile] = value

    def x_part(c, sems, where):
        return send(x_hbm.at[c], x_ref.at[f, c], sems[0].at[c], sems[1].at[c], fsdp_peer(where))

    scattered = scatter()
    far_copy = [x_part(c, (far_send, far_recv), far) for c in range(min(AHEAD, chunks))]
    for copy in mine[1:]:
        copy.start()
    sib_copy = [x_part(c, (sib_send, sib_recv), sibling) for c in range(chunks)]
    message[...] = jnp.zeros_like(message)

    def forward(c):
        far_copy[c].wait_recv()
        if len(far_copy) < chunks:
            far_copy.append(x_part(len(far_copy), (far_send, far_recv), far))
        part = x_ref.at[far, c]
        return send(part, part, fwd_send.at[c], fwd_recv.at[c], fsdp_peer(sibling))

    def wave(c, copy):
        sib_copy[c].wait_recv()
        copy.wait_recv()
        return project(c)

    copy = forward(0)
    planes = across_planes(scattered)
    for local_copy in mine[:4]:
        local_copy.wait()
    half, last = chunks // 2, chunks - 1
    summing = [wave(0, copy)]
    for c in range(1, last):
        copy = forward(c)
        if c == last - 1:
            pieces = gather_axes(planes)
        summing.append(wave(c, copy))
        finish(c - 1, summing[c - 1])
    copy = forward(last)
    summing.append(wave(last, copy))
    arriving = gather_rest(pieces)
    gradient(0, half, False)
    finish(last - 1, summing[last - 1])
    finish(last, summing[last])
    gradient(half, chunks, True)
    for local_copy in mine[4:-1]:
        local_copy.wait()
    for copy in arriving:
        copy.wait_recv()
    for copy in sent:
        copy.wait_send()


def update_kernel(
    plan_ref, delay_ref, x_ref, w_ref, dproj, stepped_ref, total, old_global, old_momentum,
    out_hbm, global_hbm, momentum_hbm, new_global, new_momentum, merged, block_sem, last_sem,
):
    height, width = total.shape
    tokens = x_ref.shape[0] * x_ref.shape[1] * x_ref.shape[2]
    plan = plan_ref[...].reshape(1, plan_ref.shape[0])
    position = plan.shape[1] - 1 - delay_ref[...].reshape(1, 1)
    chosen = lax.broadcasted_iota(jnp.int32, plan.shape, 1) == position
    fragment = jnp.sum(jnp.where(chosen, plan, 0))
    blocks = []
    for k in range(w_ref.shape[0] // height):
        here = pl.ds(k * height, height)
        blocks.append(pltpu.make_async_copy(stepped_ref.at[here], out_hbm.at[here], block_sem.at[k]))

        @pl.when(fragment != k)
        def _(k=k):
            blocks[k].start()

    replicas = GRID[0] * GRID[1] * GRID[2]
    outer_grad = old_global[...] - total[...] / replicas
    moved = outer_beta * old_momentum[...] + outer_grad
    new_momentum[...] = moved
    new_global[...] = old_global[...] - outer_rate * (outer_grad + outer_beta * moved)
    first = pl.ds(pl.multiple_of(fragment * height, height), height)
    last = [
        pltpu.make_async_copy(new_global, global_hbm, last_sem.at[0]),
        pltpu.make_async_copy(new_momentum, momentum_hbm, last_sem.at[1]),
        pltpu.make_async_copy(merged, out_hbm.at[first], last_sem.at[2]),
    ]
    for copy in last[:2]:
        copy.start()
    grad = lax.dot_general(
        x_ref[:, :, :, first].reshape(tokens, height), dproj[...].reshape(tokens, width),
        (((0,), (0,)), ((), ())), preferred_element_type=f32,
    )
    chosen = w_ref[first, :].astype(f32) - inner_rate * grad
    mixed = (1.0 - merge_weight) * chosen + merge_weight * new_global[...]
    merged[...] = mixed.astype(bf16)
    last[2].start()
    for k, copy in enumerate(blocks):

        @pl.when(fragment != k)
        def _(copy=copy):
            copy.wait()

    for copy in last:
        copy.wait()


def local(inputs, weights, cotangent, gain, snapshot, global_rows, momentum, plan, delay):
    tokens, features = inputs.shape
    width = weights.shape[1]
    height = snapshot.shape[0]
    chunks = CHUNKS
    step = tokens // chunks
    nz, ny, nx = GRID
    size = height // (nx * ny)
    most = max(nx, ny)
    hbm = pl.BlockSpec(memory_space=pltpu.HBM)
    vmem = pl.BlockSpec(memory_space=pltpu.VMEM)
    dma = pltpu.SemaphoreType.DMA

    def stay(value):
        return pltpu.with_memory_space_constraint(value, pltpu.HBM)

    kept = pl.pallas_call(
        exchange_kernel,
        name="exchange",
        out_shape=(
            pltpu.VMEM((4, chunks, step, features), bf16),
            pltpu.VMEM((features, width), bf16),
            pltpu.VMEM((4, chunks, step, width), bf16),
            pltpu.VMEM((features, width), bf16),
            pltpu.VMEM((height, width), f32),
            pltpu.VMEM((height, width), f32),
            pltpu.VMEM((height, width), f32),
        ),
        in_specs=[hbm] * 7,
        out_specs=(vmem,) * 7,
        scratch_shapes=[
            pltpu.VMEM((4, chunks, step, width), bf16),
            pltpu.VMEM((width,), f32),
            pltpu.VMEM((chunks, 4 * step, width), f32),
            pltpu.VMEM((features, width), f32),
            pltpu.VMEM((chunks, 8, 4 * step), f32),
            pltpu.VMEM((chunks, 3, 8, 4 * step), f32),
            pltpu.VMEM((nx * ny, size, width), bf16),
            pltpu.VMEM((nz, size, width), f32),
            dma((7,)),
            dma((chunks,)),
            dma((chunks,)),
            dma((chunks,)),
            dma((chunks,)),
            dma((chunks,)),
            dma((chunks,)),
            dma((chunks, 3)),
            dma((chunks, 3)),
            dma((nx * ny - 1,)),
            dma((nx * ny - 1,)),
            dma((nz - 1,)),
            dma((nz - 1,)),
            dma((2, most - 1)),
            dma((2, most - 1)),
            dma((2, most - 1, most - 1)),
            dma((2, most - 1, most - 1)),
        ],
        compiler_params=pltpu.CompilerParams(
            collective_id=0, has_side_effects=True, vmem_limit_bytes=32 * 2**20
        ),
    )(
        stay(inputs.reshape(chunks, step, features)),
        stay(weights),
        stay(cotangent.reshape(4, chunks, step, width)),
        stay(gain),
        stay(snapshot.reshape(nx * ny, size, width)),
        stay(global_rows),
        stay(momentum),
    )
    kept = [pltpu.with_memory_space_constraint(value, pltpu.VMEM) for value in kept]
    return pl.pallas_call(
        update_kernel,
        name="update",
        out_shape=(
            jax.ShapeDtypeStruct((features, width), bf16),
            jax.ShapeDtypeStruct((height, width), f32),
            jax.ShapeDtypeStruct((height, width), f32),
        ),
        in_specs=[vmem] * 9,
        out_specs=(hbm,) * 3,
        scratch_shapes=[
            pltpu.VMEM((height, width), f32),
            pltpu.VMEM((height, width), f32),
            pltpu.VMEM((height, width), bf16),
            dma((features // height,)),
            dma((3,)),
        ],
        compiler_params=pltpu.CompilerParams(vmem_limit_bytes=16 * 2**20),
    )(plan, delay, *kept)


def solution(mesh):
    in_specs = (
        P(("replica", "fsdp"), None),
        P("replica", "fsdp"),
        P("replica", "fsdp"),
        P("fsdp"),
        P("replica", "fsdp"),
        P(None, "fsdp"),
        P(None, "fsdp"),
        P(),
        P(),
    )
    out_specs = (P("replica", "fsdp"), P(None, "fsdp"), P(None, "fsdp"))
    return jax.shard_map(local, mesh=mesh, in_specs=in_specs, out_specs=out_specs, check_vma=False)
```

time: 730 us -> 40.5 us (0.06)
  the two profiles are of different devices: /device:TPU:2 before, /device:TPU:1 now
where the time goes in v2:
time: 40.5 us; the launch traced here: 40.4 us
  Pallas kernels  39.1 us (97%)
  between operations  1.32 us (3%)
    pallas_call x1, Pallas kernels, local(): pl.pallas_call(exchange_kernel, name='exchange', out_shape=(pltpu.VMEM((4...  36.2 us
    pallas_call x1, Pallas kernels, local(): pl.pallas_call(update_kernel, name='update', out_shape=(jax.ShapeDtypeStr...  2.89 us

profile of v2, /device:TPU:1, one launch (start us, length us, event | category | flops | bytes accessed | tf_op | source)
XLA Modules:
  0.0 40.4 jit_solution(13823782218878820703)
XLA Ops:
  0.6 0.0 copy-start
  1.3 36.2 %exchange.1 = (bf16[4,4,32,2048]{3,2,1,0:T(8,128)(2,1)S(1)}, bf16[2048,1152]{1,0:T(8,128)(2,1)S(1)}, bf16[4,4,32,1152]{3,2,1,0:T(8,128)(2,1)S(1)}, bf16[2048,115...) custom-call(bf16[4,32,2048]{2,1,0:T(8,128)(2,1)} %bitcast.4, ...), custom_call_target="tpu_custom_call" | custom-call | tf_op jit(solution)/shard_map/exchange/pallas_call | solution.py:332
  37.5 0.0 copy-done
  37.5 2.9 %update.1 = (bf16[2048,1152]{1,0:T(8,128)(2,1)}, f32[128,1152]{1,0:T(8,128)}, f32[128,1152]{1,0:T(8,128)}) custom-call(s32[16]{0:T(128)S(1)} %copy-done, s32[1]{0:T(128)S(6)} %copy.12.delay_ref, bf16[4,4,32,2048]{3,2,1,0:T(8,128)(2,1)S(1)} %get-tuple-element.10.x_ref, bf16[2048,1152]{1,0:T(8,128)(2,1)S(1)} %get-tuple-element.11.w_ref, ...), custom_call_target="tpu_custom_call" | custom-call | tf_op jit(solution)/shard_map/update/pallas_call | solution.py:386
Async XLA Ops:
  0.6 36.9 %copy-start = (s32[16]{0:T(128)S(1)}, s32[16]{0:T(128)}, u32[]{:S(2)}) copy-start(s32[16]{0:T(128)} %plan_ref.1) | copy-start | bytes 196

commit v3 on v2

--- a/solution.py
+++ b/solution.py
@@ -21,25 +21,18 @@
 bf16 = jnp.bfloat16
 
 
-def split_columns(width):
-    first = (width // 128 + 1) // 2 * 128
-    return ((0, first), (first, width))
-
-
 def exchange_kernel(
     x_hbm, w_hbm, cot_hbm, gain_hbm, snap_hbm, global_hbm, momentum_hbm,
-    x_ref, w_ref, dproj, stepped_ref, total, old_global, old_momentum,
-    cot, gain, proj, grad, message, sums,
+    x_ref, dproj, base, total, old_global, old_momentum,
+    w_ref, cot, gain, proj, message, sums,
     snaps, plane,
     local_sem, sib_send, sib_recv, far_send, far_recv, fwd_send, fwd_recv,
     sum_send, sum_recv, scatter_send, scatter_recv, plane_send, plane_recv,
-    axis_send, axis_recv, gather_send, gather_recv,
+    gather_send, gather_recv,
 ):
     nz, ny, nx = GRID
     r = lax.axis_index("replica")
     f = lax.axis_index("fsdp")
-    x = lax.rem(r, nx)
-    y = lax.rem(lax.div(r, nx), ny)
     z = lax.div(r, nx * ny)
     place = lax.rem(r, nx * ny)
     core = lax.rem(f, 2)
@@ -52,13 +45,6 @@
     model = 4 * width
     height = total.shape[0]
     size = height // (nx * ny)
-    columns = split_columns(width)
-
-    def x_peer(d):
-        return {"replica": r - x + lax.rem(x + d, nx)}
-
-    def y_peer(d):
-        return {"replica": r + nx * (lax.rem(y + d, ny) - y)}
 
     def plane_peer(d):
         return {"replica": r - place + lax.rem(place + d, nx * ny)}
@@ -107,60 +93,32 @@
         ]
 
     def across_planes(before):
+        mine[4].wait()
         mine[-1].wait()
         for copy in before:
             copy.wait_recv()
-        amount = snaps[0].astype(f32)
+        here = old_global[pl.ds(pl.multiple_of(place * size, size), size), :]
+        amount = here - snaps[0].astype(f32)
         for k in range(1, nx * ny):
-            amount += snaps[k].astype(f32)
-        plane[z] = amount
+            amount += here - snaps[k].astype(f32)
+        plane[z] = amount.astype(bf16)
         return [
             send(plane.at[z], plane.at[z], plane_send.at[d - 1], plane_recv.at[d - 1], z_peer(d))
             for d in range(1, nz)
         ]
 
-    def piece(k):
-        return total.at[pl.ds(pl.multiple_of(k * size, size), size)]
-
-    axes = ((nx, x_peer), (ny, y_peer))
-
-    def gather_axes(before):
+    def gather(before):
         for copy in before:
             copy.wait_recv()
-        amount = plane[0]
+        amount = plane[0].astype(f32)
         for k in range(1, nz):
-            amount += plane[k]
-        here = piece(place)
+            amount += plane[k].astype(f32)
+        here = total.at[pl.ds(pl.multiple_of(place * size, size), size)]
         here[...] = amount
         return [
-            [
-                send(here, here, axis_send.at[a, d - 1], axis_recv.at[a, d - 1], peer(d))
-                for d in range(1, n)
-            ]
-            for a, (n, peer) in enumerate(axes)
+            send(here, here, gather_send.at[d - 1], gather_recv.at[d - 1], plane_peer(d))
+            for d in range(1, nx * ny)
         ]
-
-    def gather_rest(before):
-        arriving = []
-        most = max(nx, ny)
-        for d in sorted(range(1, most), key=lambda d: min(d, most - d)):
-            for a, (n, _) in enumerate(axes):
-                if d >= n:
-                    continue
-                before[a][d - 1].wait_recv()
-                from_x = place - x + lax.rem(x + nx - d, nx)
-                from_y = place + nx * (lax.rem(y + ny - d, ny) - y)
-                lo, hi = columns[1 - a]
-                part = piece((from_x, from_y)[a]).at[:, pl.ds(lo, hi - lo)]
-                m, peer = axes[1 - a]
-                for e in range(1, m):
-                    arriving.append(
-                        send(
-                            part, part,
-                            gather_send.at[a, d - 1, e - 1], gather_recv.at[a, d - 1, e - 1], peer(e),
-                        )
-                    )
-        return arriving
 
     def scaled_of(c):
         return cot[:, c].reshape(rows, width).astype(f32) * (1.0 + gain[...].reshape(1, width))
@@ -199,20 +157,16 @@
             value = inverse * scaled[:, k : k + 128] - proj[c, :, k : k + 128] * factor
             dproj[:, c, :, k : k + 128] = value.astype(bf16).reshape(4, step, 128)
 
-    def gradient(first, last, final):
-        count = last - first
-        right = dproj[:, first:last].reshape(count * rows, width)
+    def begin_update():
+        half = chunks // 2
+        right = dproj[:, :half].reshape(half * rows, width)
         tile = min(256, features)
         for k in range(0, features, tile):
-            left = x_ref[:, first:last, :, k : k + tile].reshape(count * rows, tile)
+            left = x_ref[:, :half, :, k : k + tile].reshape(half * rows, tile)
             value = lax.dot_general(
                 left, right, (((0,), (0,)), ((), ())), preferred_element_type=f32
             )
-            if final:
-                value = w_ref[k : k + tile].astype(f32) - inner_rate * (grad[k : k + tile] + value)
-                stepped_ref[k : k + tile] = value.astype(bf16)
-            else:
-                grad[k : k + tile] = value
+            base[k : k + tile] = w_ref[k : k + tile].astype(f32) - inner_rate * value
 
     def x_part(c, sems, where):
         return send(x_hbm.at[c], x_ref.at[f, c], sems[0].at[c], sems[1].at[c], fsdp_peer(where))
@@ -240,50 +194,62 @@
     planes = across_planes(scattered)
     for local_copy in mine[:4]:
         local_copy.wait()
-    half, last = chunks // 2, chunks - 1
+    last = chunks - 1
     summing = [wave(0, copy)]
-    for c in range(1, last):
-        copy = forward(c)
-        if c == last - 1:
-            pieces = gather_axes(planes)
-        summing.append(wave(c, copy))
-        finish(c - 1, summing[c - 1])
+    copy = forward(1)
+    summing.append(wave(1, copy))
+    finish(0, summing[0])
+    copy = forward(2)
+    pieces = gather(planes)
+    summing.append(wave(2, copy))
+    finish(1, summing[1])
     copy = forward(last)
     summing.append(wave(last, copy))
-    arriving = gather_rest(pieces)
-    gradient(0, half, False)
+    begin_update()
     finish(last - 1, summing[last - 1])
     finish(last, summing[last])
-    gradient(half, chunks, True)
-    for local_copy in mine[4:-1]:
+    for local_copy in mine[5:-1]:
         local_copy.wait()
-    for copy in arriving:
+    for copy in pieces:
         copy.wait_recv()
     for copy in sent:
         copy.wait_send()
 
 
 def update_kernel(
-    plan_ref, delay_ref, x_ref, w_ref, dproj, stepped_ref, total, old_global, old_momentum,
-    out_hbm, global_hbm, momentum_hbm, new_global, new_momentum, merged, block_sem, last_sem,
+    plan_ref, delay_ref, x_ref, dproj, base, total, old_global, old_momentum,
+    out_hbm, global_hbm, momentum_hbm, stepped, new_global, new_momentum, merged, block_sem, last_sem,
 ):
     height, width = total.shape
-    tokens = x_ref.shape[0] * x_ref.shape[1] * x_ref.shape[2]
+    features = base.shape[0]
+    _, chunks, step, _ = x_ref.shape
+    half = chunks // 2
+    rows = 4 * (chunks - half) * step
     plan = plan_ref[...].reshape(1, plan_ref.shape[0])
     position = plan.shape[1] - 1 - delay_ref[...].reshape(1, 1)
     chosen = lax.broadcasted_iota(jnp.int32, plan.shape, 1) == position
     fragment = jnp.sum(jnp.where(chosen, plan, 0))
+    right = dproj[:, half:].reshape(rows, width)
+
+    def finished(here, count):
+        left = x_ref[:, half:, :, here].reshape(rows, count)
+        grad = lax.dot_general(left, right, (((0,), (0,)), ((), ())), preferred_element_type=f32)
+        return base[here, :] - inner_rate * grad
+
+    tile = min(256, features)
     blocks = []
-    for k in range(w_ref.shape[0] // height):
-        here = pl.ds(k * height, height)
-        blocks.append(pltpu.make_async_copy(stepped_ref.at[here], out_hbm.at[here], block_sem.at[k]))
-
-        @pl.when(fragment != k)
-        def _(k=k):
-            blocks[k].start()
+    for i in range(0, features, tile):
+        stepped[i : i + tile] = finished(pl.ds(i, tile), tile).astype(bf16)
+        for k in range(i // height, (i + tile) // height):
+            here = pl.ds(k * height, height)
+            blocks.append(pltpu.make_async_copy(stepped.at[here], out_hbm.at[here], block_sem.at[k]))
+
+            @pl.when(fragment != k)
+            def _(k=k):
+                blocks[k].start()
 
     replicas = GRID[0] * GRID[1] * GRID[2]
-    outer_grad = old_global[...] - total[...] / replicas
+    outer_grad = total[...] / replicas
     moved = outer_beta * old_momentum[...] + outer_grad
     new_momentum[...] = moved
     new_global[...] = old_global[...] - outer_rate * (outer_grad + outer_beta * moved)
@@ -295,12 +261,7 @@
     ]
     for copy in last[:2]:
         copy.start()
-    grad = lax.dot_general(
-        x_ref[:, :, :, first].reshape(tokens, height), dproj[...].reshape(tokens, width),
-        (((0,), (0,)), ((), ())), preferred_element_type=f32,
-    )
-    chosen = w_ref[first, :].astype(f32) - inner_rate * grad
-    mixed = (1.0 - merge_weight) * chosen + merge_weight * new_global[...]
+    mixed = (1.0 - merge_weight) * finished(first, height) + merge_weight * new_global[...]
     merged[...] = mixed.astype(bf16)
     last[2].start()
     for k, copy in enumerate(blocks):
@@ -321,7 +282,6 @@
     step = tokens // chunks
     nz, ny, nx = GRID
     size = height // (nx * ny)
-    most = max(nx, ny)
     hbm = pl.BlockSpec(memory_space=pltpu.HBM)
     vmem = pl.BlockSpec(memory_space=pltpu.VMEM)
     dma = pltpu.SemaphoreType.DMA
@@ -334,24 +294,23 @@
         name="exchange",
         out_shape=(
             pltpu.VMEM((4, chunks, step, features), bf16),
-            pltpu.VMEM((features, width), bf16),
             pltpu.VMEM((4, chunks, step, width), bf16),
-            pltpu.VMEM((features, width), bf16),
+            pltpu.VMEM((features, width), f32),
             pltpu.VMEM((height, width), f32),
             pltpu.VMEM((height, width), f32),
             pltpu.VMEM((height, width), f32),
         ),
         in_specs=[hbm] * 7,
-        out_specs=(vmem,) * 7,
+        out_specs=(vmem,) * 6,
         scratch_shapes=[
+            pltpu.VMEM((features, width), bf16),
             pltpu.VMEM((4, chunks, step, width), bf16),
             pltpu.VMEM((width,), f32),
             pltpu.VMEM((chunks, 4 * step, width), f32),
-            pltpu.VMEM((features, width), f32),
             pltpu.VMEM((chunks, 8, 4 * step), f32),
             pltpu.VMEM((chunks, 3, 8, 4 * step), f32),
             pltpu.VMEM((nx * ny, size, width), bf16),
-            pltpu.VMEM((nz, size, width), f32),
+            pltpu.VMEM((nz, size, width), bf16),
             dma((7,)),
             dma((chunks,)),
             dma((chunks,)),
@@ -365,10 +324,8 @@
             dma((nx * ny - 1,)),
             dma((nz - 1,)),
             dma((nz - 1,)),
-            dma((2, most - 1)),
-            dma((2, most - 1)),
-            dma((2, most - 1, most - 1)),
-            dma((2, most - 1, most - 1)),
+            dma((nx * ny - 1,)),
+            dma((nx * ny - 1,)),
         ],
         compiler_params=pltpu.CompilerParams(
             collective_id=0, has_side_effects=True, vmem_limit_bytes=32 * 2**20
@@ -391,9 +348,10 @@
             jax.ShapeDtypeStruct((height, width), f32),
             jax.ShapeDtypeStruct((height, width), f32),
         ),
-        in_specs=[vmem] * 9,
+        in_specs=[vmem] * 8,
         out_specs=(hbm,) * 3,
         scratch_shapes=[
+            pltpu.VMEM((features, width), bf16),
             pltpu.VMEM((height, width), f32),
             pltpu.VMEM((height, width), f32),
             pltpu.VMEM((height, width), bf16),

time: 40.5 us -> 37.3 us (0.921)
  Pallas kernels: 39.1 us -> 35.8 us
    pallas_call x1, Pallas kernels: 36.2 us -> 32.5 us  [local(): pl.pallas_call(exchange_kernel, name='exchange', out_shape=(pltpu.VMEM((4...]
where the time goes in v3:
time: 37.3 us; the launch traced here: 37.1 us
  Pallas kernels  35.8 us (96%)
  between operations  1.32 us (4%)
    pallas_call x1, Pallas kernels, local(): pl.pallas_call(exchange_kernel, name='exchange', out_shape=(pltpu.VMEM((4...  32.5 us
    pallas_call x1, Pallas kernels, local(): pl.pallas_call(update_kernel, name='update', out_shape=(jax.ShapeDtypeStr...  3.23 us

profile of v3, /device:TPU:1, one launch (start us, length us, event | category | flops | bytes accessed | tf_op | source)
XLA Modules:
  0.0 37.1 jit_solution(5924422159137437091)
XLA Ops:
  0.6 0.0 copy-start
  1.3 32.5 %exchange.1 = (bf16[4,4,32,2048]{3,2,1,0:T(8,128)(2,1)S(1)}, bf16[4,4,32,1152]{3,2,1,0:T(8,128)(2,1)S(1)}, f32[2048,1152]{1,0:T(8,128)S(1)}, f32[128,1152]{1,0:T...) custom-call(bf16[4,32,2048]{2,1,0:T(8,128)(2,1)} %bitcast.4, bf16[2048,1152]{1,0:T(8,128)(2,1)} %w_hbm.1, ...), custom_call_target="tpu_custom_call" | custom-call | tf_op jit(solution)/shard_map/exchange/pallas_call | solution.py:292
  33.9 0.0 copy-done
  33.9 3.2 %update.1 = (bf16[2048,1152]{1,0:T(8,128)(2,1)}, f32[128,1152]{1,0:T(8,128)}, f32[128,1152]{1,0:T(8,128)}) custom-call(s32[16]{0:T(128)S(1)} %copy-done, s32[1]{0:T(128)S(6)} %copy.12.delay_ref, bf16[4,4,32,2048]{3,2,1,0:T(8,128)(2,1)S(1)} %get-tuple-element.9.x_ref, bf16[4,4,32,1152]{3,2,1,0:T(8,128)(2,1)S(1)} %get-tuple-element.10.dproj, ...), custom_call_target="tpu_custom_call" | custom-call | tf_op jit(solution)/shard_map/update/pallas_call | solution.py:343
Async XLA Ops:
  0.6 33.2 %copy-start = (s32[16]{0:T(128)S(1)}, s32[16]{0:T(128)}, u32[]{:S(2)}) copy-start(s32[16]{0:T(128)} %plan_ref.1) | copy-start | bytes 196

commit v4 on v3

--- a/solution.py
+++ b/solution.py
@@ -15,7 +15,8 @@
 
 GRID = (4, 4, 4)
 CHUNKS = 4
-AHEAD = 2
+AHEAD = 3
+PARTS = 2
 
 f32 = jnp.float32
 bf16 = jnp.bfloat16
@@ -168,26 +169,43 @@
             )
             base[k : k + tile] = w_ref[k : k + tile].astype(f32) - inner_rate * value
 
-    def x_part(c, sems, where):
-        return send(x_hbm.at[c], x_ref.at[f, c], sems[0].at[c], sems[1].at[c], fsdp_peer(where))
+    piece = step // PARTS
+    parts = chunks * PARTS
+
+    def lines(p):
+        return p // PARTS, pl.ds(p % PARTS * piece, piece)
+
+    def x_part(p):
+        c, here = lines(p)
+        return send(
+            x_hbm.at[c, here], x_ref.at[f, c, here], far_send.at[p], far_recv.at[p], fsdp_peer(far)
+        )
+
+    def x_chunk(c):
+        return send(x_hbm.at[c], x_ref.at[f, c], sib_send.at[c], sib_recv.at[c], fsdp_peer(sibling))
 
     scattered = scatter()
-    far_copy = [x_part(c, (far_send, far_recv), far) for c in range(min(AHEAD, chunks))]
+    far_copy = [x_part(p) for p in range(min(AHEAD, parts))]
     for copy in mine[1:]:
         copy.start()
-    sib_copy = [x_part(c, (sib_send, sib_recv), sibling) for c in range(chunks)]
+    sib_copy = [x_chunk(c) for c in range(chunks)]
     message[...] = jnp.zeros_like(message)
 
+    def pass_on(p):
+        far_copy[p].wait_recv()
+        if len(far_copy) < parts:
+            far_copy.append(x_part(len(far_copy)))
+        c, here = lines(p)
+        part = x_ref.at[far, c, here]
+        return send(part, part, fwd_send.at[p], fwd_recv.at[p], fsdp_peer(sibling))
+
     def forward(c):
-        far_copy[c].wait_recv()
-        if len(far_copy) < chunks:
-            far_copy.append(x_part(len(far_copy), (far_send, far_recv), far))
-        part = x_ref.at[far, c]
-        return send(part, part, fwd_send.at[c], fwd_recv.at[c], fsdp_peer(sibling))
-
-    def wave(c, copy):
+        return [pass_on(p) for p in range(c * PARTS, (c + 1) * PARTS)]
+
+    def wave(c, copies):
         sib_copy[c].wait_recv()
-        copy.wait_recv()
+        for copy in copies:
+            copy.wait_recv()
         return project(c)
 
     copy = forward(0)
@@ -314,10 +332,10 @@
             dma((7,)),
             dma((chunks,)),
             dma((chunks,)),
-            dma((chunks,)),
-            dma((chunks,)),
-            dma((chunks,)),
-            dma((chunks,)),
+            dma((chunks * PARTS,)),
+            dma((chunks * PARTS,)),
+            dma((chunks * PARTS,)),
+            dma((chunks * PARTS,)),
             dma((chunks, 3)),
             dma((chunks, 3)),
             dma((nx * ny - 1,)),

time: 37.3 us -> 35.8 us (0.960); the launches traced: 37.1 us -> 35.2 us
  Pallas kernels: 35.8 us -> 33.9 us
    pallas_call x1, Pallas kernels: 32.5 us -> 30.7 us  [local(): pl.pallas_call(exchange_kernel, name='exchange', out_shape=(pltpu.VMEM((4...]
where the time goes in v4:
time: 35.8 us; the launch traced here: 35.2 us
  Pallas kernels  33.9 us (95%)
  between operations  1.32 us (4%)
    pallas_call x1, Pallas kernels, local(): pl.pallas_call(exchange_kernel, name='exchange', out_shape=(pltpu.VMEM((4...  30.7 us
    pallas_call x1, Pallas kernels, local(): pl.pallas_call(update_kernel, name='update', out_shape=(jax.ShapeDtypeStr...  3.21 us

profile of v4, /device:TPU:1, one launch (start us, length us, event | category | flops | bytes accessed | tf_op | source)
XLA Modules:
  0.0 35.2 jit_solution(4663984732426479569)
XLA Ops:
  0.6 0.0 copy-start
  1.3 30.7 %exchange.1 = (bf16[4,4,32,2048]{3,2,1,0:T(8,128)(2,1)S(1)}, bf16[4,4,32,1152]{3,2,1,0:T(8,128)(2,1)S(1)}, f32[2048,1152]{1,0:T(8,128)S(1)}, f32[128,1152]{1,0:T...) custom-call(bf16[4,32,2048]{2,1,0:T(8,128)(2,1)} %bitcast.4, bf16[2048,1152]{1,0:T(8,128)(2,1)} %w_hbm.1, ...), custom_call_target="tpu_custom_call" | custom-call | tf_op jit(solution)/shard_map/exchange/pallas_call | solution.py:310
  32.0 0.0 copy-done
  32.0 3.2 %update.1 = (bf16[2048,1152]{1,0:T(8,128)(2,1)}, f32[128,1152]{1,0:T(8,128)}, f32[128,1152]{1,0:T(8,128)}) custom-call(s32[16]{0:T(128)S(1)} %copy-done, s32[1]{0:T(128)S(6)} %copy.12.delay_ref, bf16[4,4,32,2048]{3,2,1,0:T(8,128)(2,1)S(1)} %get-tuple-element.9.x_ref, bf16[4,4,32,1152]{3,2,1,0:T(8,128)(2,1)S(1)} %get-tuple-element.10.dproj, ...), custom_call_target="tpu_custom_call" | custom-call | tf_op jit(solution)/shard_map/update/pallas_call | solution.py:361
Async XLA Ops:
  0.6 31.3 %copy-start = (s32[16]{0:T(128)S(1)}, s32[16]{0:T(128)}, u32[]{:S(2)}) copy-start(s32[16]{0:T(128)} %plan_ref.1) | copy-start | bytes 196

commit v5 on v4

--- a/solution.py
+++ b/solution.py
@@ -47,8 +47,15 @@
     height = total.shape[0]
     size = height // (nx * ny)
 
+    x, y = lax.rem(place, nx), lax.div(place, nx)
+    hops = [min(d % nx, nx - d % nx) + min(d // nx, ny - d // nx) for d in range(nx * ny)]
+    farthest_first = sorted(range(1, nx * ny), key=lambda d: -hops[d])
+
+    def plane_place(d):
+        return lax.rem(x + d % nx, nx) + nx * lax.rem(y + d // nx, ny)
+
     def plane_peer(d):
-        return {"replica": r - place + lax.rem(place + d, nx * ny)}
+        return {"replica": r - place + plane_place(d)}
 
     def z_peer(d):
         return {"replica": r + nx * ny * (lax.rem(z + d, nz) - z)}
@@ -87,10 +94,10 @@
     def scatter():
         return [
             send(
-                snap_hbm.at[lax.rem(place + d, nx * ny)], snaps.at[d],
+                snap_hbm.at[plane_place(d)], snaps.at[d],
                 scatter_send.at[d - 1], scatter_recv.at[d - 1], plane_peer(d),
             )
-            for d in range(1, nx * ny)
+            for d in farthest_first
         ]
 
     def across_planes(before):
@@ -118,7 +125,7 @@
         here[...] = amount
         return [
             send(here, here, gather_send.at[d - 1], gather_recv.at[d - 1], plane_peer(d))
-            for d in range(1, nx * ny)
+            for d in farthest_first
         ]
 
     def scaled_of(c):

time: 35.8 us -> 35.8 us (level); the launches traced: 35.2 us -> 35.7 us
  Pallas kernels: 33.9 us -> 34.4 us
    pallas_call x1, Pallas kernels: 30.7 us -> 31.2 us  [local(): pl.pallas_call(exchange_kernel, name='exchange', out_shape=(pltpu.VMEM((4...]
where the time goes in v5:
time: 35.8 us; the launch traced here: 35.7 us
  Pallas kernels  34.4 us (96%)
  between operations  1.32 us (4%)
    pallas_call x1, Pallas kernels, local(): pl.pallas_call(exchange_kernel, name='exchange', out_shape=(pltpu.VMEM((4...  31.2 us
    pallas_call x1, Pallas kernels, local(): pl.pallas_call(update_kernel, name='update', out_shape=(jax.ShapeDtypeStr...  3.22 us

profile of v5, /device:TPU:1, one launch (start us, length us, event | category | flops | bytes accessed | tf_op | source)
XLA Modules:
  0.0 35.7 jit_solution(2613381369363496864)
XLA Ops:
  0.6 0.0 copy-start
  1.3 31.2 %exchange.1 = (bf16[4,4,32,2048]{3,2,1,0:T(8,128)(2,1)S(1)}, bf16[4,4,32,1152]{3,2,1,0:T(8,128)(2,1)S(1)}, f32[2048,1152]{1,0:T(8,128)S(1)}, f32[128,1152]{1,0:T...) custom-call(bf16[4,32,2048]{2,1,0:T(8,128)(2,1)} %bitcast.4, bf16[2048,1152]{1,0:T(8,128)(2,1)} %w_hbm.1, ...), custom_call_target="tpu_custom_call" | custom-call | tf_op jit(solution)/shard_map/exchange/pallas_call | solution.py:317
  32.5 0.0 copy-done
  32.5 3.2 %update.1 = (bf16[2048,1152]{1,0:T(8,128)(2,1)}, f32[128,1152]{1,0:T(8,128)}, f32[128,1152]{1,0:T(8,128)}) custom-call(s32[16]{0:T(128)S(1)} %copy-done, s32[1]{0:T(128)S(6)} %copy.12.delay_ref, bf16[4,4,32,2048]{3,2,1,0:T(8,128)(2,1)S(1)} %get-tuple-element.9.x_ref, bf16[4,4,32,1152]{3,2,1,0:T(8,128)(2,1)S(1)} %get-tuple-element.10.dproj, ...), custom_call_target="tpu_custom_call" | custom-call | tf_op jit(solution)/shard_map/update/pallas_call | solution.py:368
Async XLA Ops:
  0.6 31.9 %copy-start = (s32[16]{0:T(128)S(1)}, s32[16]{0:T(128)}, u32[]{:S(2)}) copy-start(s32[16]{0:T(128)} %plan_ref.1) | copy-start | bytes 196
